TPU v7x, 32 devices: a whole 2x2x4 slice. The times are simulated.
32 devices in a mesh: lon: 16 (over z, y, core), plane: 2 (over x).
Axes of the slice: x: 2, y: 2, z: 4, core: 2. Of those that a mesh axis runs over, the one named last changes fastest.
Arguments:
- potential: float32 [2, 256, 4096], P('plane', None, 'lon'), may hold values from -0.6 to 0.6
- lens_weight: float32 [2, 2], P('plane'), may hold values from 0.1 to 0.3
- cycle_shift: int32 [2, 256], replicated, may hold values from -3 to 2
- cycle_weight: int32 [2, 256], replicated, may hold values from 0 to 16
- cycle_scale: float32 [256], replicated, may hold values from 1 to 2
Outputs:
- displacement: float32 [2, 2, 256, 4096], P('plane', None, None, 'lon')
- jacobian: float32 [2, 4, 256, 4096], P('plane', None, None, 'lon')
All inputs are finite; a program needn't handle non-finite values.
Results may differ from a plain program's by a relative error of at most 0.00002.
Values sent between devices are 32-bit elements; how exact they have to be, the bound alone decides.
A program may use at most 64 MiB of HBM per device.

v0:
```python
import jax
import jax.numpy as jnp
from jax import lax
from jax.sharding import PartitionSpec as P

HALO = 4


def shifted(value, axis, steps):
    count = lax.axis_size(axis)
    pairs = [(source, (source + steps) % count) for source in range(count)]
    return lax.ppermute(value, axis, pairs)


def extended(block, sides, width):
    for axis, dim in sides:
        count = lax.axis_size(axis)
        forward = [(i, i + 1) for i in range(count - 1)]
        forward.append((count - 1, 0))
        backward = [(target, source) for source, target in forward]
        low = lax.ppermute(
            lax.slice_in_dim(block, block.shape[dim] - width, None, axis=dim), axis, forward
        )
        high = lax.ppermute(lax.slice_in_dim(block, 0, width, axis=dim), axis, backward)
        block = jnp.concatenate([low, block, high], axis=dim)
    return block


def from_root(shard, axis, root):
    mine = lax.axis_index(axis) == root
    return lax.psum(jnp.where(mine, shard, jnp.zeros_like(shard)), axis)


def pick_cycle(row_block, shifts, offset, width):
    result = jnp.zeros((row_block.shape[0], width), jnp.float32)
    for delta in range(-3, 3):
        start = HALO + delta + offset
        result = jnp.where(shifts[:, None] == delta, row_block[:, start : start + width], result)
    return result


def cycle_value(row_block, shifts, weights, offset, width):
    frac = weights.astype(jnp.float32)[:, None] / 16.0
    first = pick_cycle(row_block, shifts, offset, width)
    second = pick_cycle(row_block, shifts, offset + 1, width)
    return (1.0 - frac) * first + frac * second


def derivatives(padded, cycle_shift, cycle_weight, cycle_scale):
    width = padded.shape[1] - 2 * HALO
    north_rows = padded[:-2]
    south_rows = padded[2:]
    middle = padded[1:-1]
    north = [
        cycle_value(north_rows, cycle_shift[0], cycle_weight[0], offset, width)
        for offset in (-1, 0, 1)
    ]
    south = [
        cycle_value(south_rows, cycle_shift[1], cycle_weight[1], offset, width)
        for offset in (-1, 0, 1)
    ]
    center = [middle[:, HALO + offset : HALO + offset + width] for offset in (-1, 0, 1)]
    metric = cycle_scale[:, None]
    alpha_t = 0.5 * (south[1] - north[1])
    alpha_p = 0.5 * metric * (center[2] - center[0])
    shear_tt = south[1] - 2.0 * center[1] + north[1]
    shear_pp = metric * metric * (center[2] - 2.0 * center[1] + center[0])
    shear_tp = 0.25 * metric * (south[2] - south[0] - north[2] + north[0])
    return (alpha_t, alpha_p, shear_tt, shear_pp, shear_tp)


def advance(state, fields, gain):
    disp_t, disp_p, a_zz, a_zo, a_oz, a_oo = state
    alpha_t, alpha_p, shear_tt, shear_pp, shear_tp = fields
    new_t = disp_t - gain * (alpha_t + shear_tt * disp_t + shear_tp * disp_p)
    new_p = disp_p - gain * (alpha_p + shear_tp * disp_t + shear_pp * disp_p)
    b_zz = a_zz - gain * (shear_tt * a_zz + shear_tp * a_oz)
    b_zo = a_zo - gain * (shear_tt * a_zo + shear_tp * a_oo)
    b_oz = a_oz - gain * (shear_tp * a_zz + shear_pp * a_oz)
    b_oo = a_oo - gain * (shear_tp * a_zo + shear_pp * a_oo)
    return (new_t, new_p, b_zz, b_zo, b_oz, b_oo)


def pad_rows(tile):
    return jnp.pad(tile, ((1, 1), (0, 0)))


def per_device(potential, lens_weight, cycle_shift, cycle_weight, cycle_scale):
    planes = lax.axis_size("plane")
    lon_count = lax.axis_size("lon")
    by_tiles = lon_count - lon_count // 4
    rows_count = potential.shape[1]
    width = potential.shape[2]
    gains = lens_weight[0]
    zeros = jnp.zeros((rows_count, width), jnp.float32)
    ones = jnp.ones((rows_count, width), jnp.float32)
    state = (zeros, zeros, ones, zeros, zeros, ones)
    for plane_k in range(planes):
        turned = shifted(from_root(potential, "plane", plane_k), "lon", by_tiles)
        sky_tile = extended(turned, (("lon", 2),), HALO)[0]
        fields = derivatives(pad_rows(sky_tile), cycle_shift, cycle_weight, cycle_scale)
        state = advance(state, fields, gains[plane_k])
    displacement = jnp.stack(state[0:2])[None]
    jacobian = jnp.stack(state[2:6])[None]
    return (displacement, jacobian)


def solution(mesh):
    in_specs = (P("plane", None, "lon"), P("plane", None), P(), P(), P())
    out_specs = (P("plane", None, None, "lon"), P("plane", None, None, "lon"))
    return jax.shard_map(
        per_device, mesh=mesh, in_specs=in_specs, out_specs=out_specs, check_vma=False
    )
```

profile of v0, /device:TPU:0, one launch (start us, length us, event | category | flops | bytes accessed | tf_op | source)
XLA Modules:
  0.0 84.2 jit_solution(8897131879837512559)
XLA Ops:
  7.2 0.0 all-reduce.5.cloned.1.call-start
  7.2 1.8 %broadcast_select_fusion = (f32[1,256,256]{2,1,0:T(8,128)}, f32[1,256,256]{2,1,0:T(8,128)}) fusion(f32[1,256,256]{2,1,0:T(8,128)} %param.5, pred[]{:T(512)S(6)} %eq.295, pred[]{:T(512)S(6)} %eq.126), kind=kLoop, calls=%fused_computation.50 | loop fusion | flops 131072 | bytes 786434 | tf_op jit(solution)/shard_map/jit(_where)/select_n | solution.py:31
  9.0 0.0 copy-start
  9.0 0.0 all-reduce.5.cloned.1.call-update
  9.0 0.7 copy-done
  9.7 0.0 copy-start.3
  9.7 0.7 copy-done.3
  10.4 32.1 %all-reduce.5.cloned.1.call-done = (f32[1,256,256]{2,1,0:T(8,128)}, f32[1,256,256]{2,1,0:T(8,128)}) async-done(((f32[1,256,256]{2,1,0:T(8,128)}, f32[1,256,256]{2,1,0:T(8,128)}), (f32[1,256,256]{2,1,0:T(8,128)}, f32[1,256,256]{2,1,0:T(8,128)})) %all-reduce.5.cloned.1.call-update) | async-done | bytes 524304 | tf_op jit(solution)/shard_map/psum | solution.py:31
  42.4 3.3 %collective-permute-start = (f32[1,256,256]{2,1,0:T(8,128)}, f32[1,256,256]{2,1,0:T(8,128)S(1)}, u32[]{:S(2)}, u32[]{:S(2)}) collective-permute-start(f32[1,256,256]{2,1,0:T(8,128)} %get-tuple-element.14), channel_id=1, source_target_pairs={{0,24},{2,26},{4,28},{6,30},{8,0},{10,2},{12,4},{14,6},{16,8},{18,... | collective-permute-start | bytes 786440 | tf_op jit(solution)/shard_map/ppermute | solution.py:12
  45.8 0.0 copy-start.2
  45.8 0.7 copy-done.2
  46.5 0.0 copy-start.1
  46.5 0.6 collective-permute-start.3
  47.1 0.1 copy-done.1
  47.1 0.6 fusion.2
  47.7 5.1 %collective-permute-done = f32[1,256,256]{2,1,0:T(8,128)S(1)} collective-permute-done((f32[1,256,256]{2,1,0:T(8,128)}, f32[1,256,256]{2,1,0:T(8,128)S(1)}, u32[]{:S(2)}, u32[]{:S(2)}) %collective-permute-start) | collective-permute-done | bytes 262176 | tf_op jit(solution)/shard_map/ppermute | solution.py:12
  52.8 0.1 fusion
  52.9 0.1 collective-permute-start.1
  52.9 4.4 %collective-permute-start.2 = (f32[1,256,4]{2,1,0:T(8,128)S(1)}, f32[1,256,4]{2,1,0:T(8,128)S(1)}, u32[]{:S(2)}, u32[]{:S(2)}) collective-permute-start(f32[1,256,4]{2,1,0:T(8,128)S(1)} %get-tuple-element.38), channel_id=1, source_target_pairs={{2,0},{4,2},{6,4},{8,6},{10,8},{12,10},{14,12},{16,14},{18,16},{20... | collective-permute-start | bytes 12296 | tf_op jit(solution)/shard_map/ppermute | solution.py:24
  57.4 0.0 collective-permute-done.3
  57.4 0.1 fusion.1
  57.5 0.1 collective-permute-start.4
  57.5 4.4 %collective-permute-start.5 = (f32[1,256,4]{2,1,0:T(8,128)S(1)}, f32[1,256,4]{2,1,0:T(8,128)S(1)}, u32[]{:S(2)}, u32[]{:S(2)}) collective-permute-start(f32[1,256,4]{2,1,0:T(8,128)S(1)} %get-tuple-element.40), channel_id=1, source_target_pairs={{2,0},{4,2},{6,4},{8,6},{10,8},{12,10},{14,12},{16,14},{18,16},{20... | collective-permute-start | bytes 12296 | tf_op jit(solution)/shard_map/ppermute | solution.py:24
  62.0 0.0 collective-permute-done.1
  62.0 0.0 collective-permute-done.2
  62.0 0.2 maximum_bitcast_fusion.2
  62.2 2.5 %collective-permute-done.4 = f32[1,256,4]{2,1,0:T(8,128)S(1)} collective-permute-done((f32[1,256,4]{2,1,0:T(8,128)S(1)}, f32[1,256,4]{2,1,0:T(8,128)S(1)}, u32[]{:S(2)}, u32[]{:S(2)}) %collective-permute-start.4) | collective-permute-done | bytes 4128 | tf_op jit(solution)/shard_map/ppermute | solution.py:21
  64.7 0.0 collective-permute-done.5
  64.7 0.2 maximum_bitcast_fusion.3
  64.9 6.9 %subtract_bitcast_fusion.3 = (f32[1,256,256]{2,1,0:T(8,128)S(1)}, f32[256,256]{1,0:T(8,128)S(1)}, f32[256,256]{1,0:T(8,128)S(1)}, f32[256,256]{1,0:T(8,128)S(1)}...) fusion(f32[]{:T(128)} %bitcast.4, f32[]{:T(128)} %bitcast, ...), kind=kLoop, calls=%fused_computation.11 | loop fusion | flops 13762560 | bytes 4206600 | tf_op jit(solution)/shard_map/stack | solution.py:104
  71.9 2.0 %subtract_bitcast_fusion.1 = (f32[1,256,256]{2,1,0:T(8,128)S(1)}, f32[256,256]{1,0:T(8,128)S(1)}, f32[1,256,256]{2,1,0:T(8,128)S(1)}, f32[1,256,256]{2,1,0:T(8,1...) fusion(f32[256,256]{1,0:T(8,128)S(1)} %get-tuple-element.22, f32[]{:T(128)} %bitcast.4, ...), kind=kLoop, calls=%fused_computation.7 | loop fusion | flops 3342336 | bytes 4982792 | tf_op jit(solution)/shard_map/stack | solution.py:104
  73.9 1.6 %subtract_bitcast_fusion = (f32[1,256,256]{2,1,0:T(8,128)S(1)}, f32[1,256,256]{2,1,0:T(8,128)S(1)}) fusion(f32[256,256]{1,0:T(8,128)S(1)} %get-tuple-element.26, f32[256,256]{1,0:T(8,128)S(1)} %get-tuple-element.22, f32[]{:T(128)} %bitcast.4, f32[256,256]{1,0:T(8,128)S(1)} %get-tuple-element.23, f32[256,256]{1,0:T(8,128)S(1)} %get-tuple-element.19, f32[]{:T(128)} %bitcast, ...), kind=kLoop, calls=%fused_computation.6 | loop fusion | flops 1376256 | bytes 2884616 | tf_op jit(solution)/shard_map/stack | solution.py:104
  75.5 0.8 maximum_bitcast_fusion.1
  76.3 1.0 %maximum_bitcast_fusion = f32[1,4,256,256]{3,2,1,0:T(8,128)} fusion(f32[1,256,256]{2,1,0:T(8,128)S(1)} %get-tuple-element.35, f32[1,256,256]{2,1,0:T(8,128)S(1)} %get-tuple-element.25, f32[1,256,256]{2,1,0:T(8,128)S(1)} %get-tuple-element.31, f32[1,256,256]{2,1,0:T(8,128)S(1)} %get-tuple-element.16), kind=kLoop, calls=%fused_computation | loop fusion | flops 786432 | bytes 2097152 | tf_op jit(solution)/shard_map/broadcast_in_dim | solution.py:104
  (4 shorter events, 0.1 us)
Async XLA Ops:
  7.2 35.3 %all-reduce.5.cloned.1.call-start = ((), (), s32[]{:S(2)}) async-start(), calls=%async_computation | async-start | bytes 1048576 | tf_op jit(solution)/shard_map/psum | solution.py:31
  9.0 0.7 copy-start
  9.7 0.7 copy-start.3
  42.4 10.4 %collective-permute-start = (f32[1,256,256]{2,1,0:T(8,128)}, f32[1,256,256]{2,1,0:T(8,128)S(1)}, u32[]{:S(2)}, u32[]{:S(2)}) collective-permute-start(f32[1,256,256]{2,1,0:T(8,128)} %get-tuple-element.14), channel_id=1, source_target_pairs={{0,24},{2,26},{4,28},{6,30},{8,0},{10,2},{12,4},{14,6},{16,8},{18,... | collective-permute-start | bytes 786440 | tf_op jit(solution)/shard_map/ppermute | solution.py:12
  45.8 0.7 copy-start.2
  46.5 0.7 copy-start.1
  46.5 10.9 %collective-permute-start.3 = (f32[1,256,256]{2,1,0:T(8,128)}, f32[1,256,256]{2,1,0:T(8,128)S(1)}, u32[]{:S(2)}, u32[]{:S(2)}) collective-permute-start(f32[1,256,256]{2,1,0:T(8,128)} %get-tuple-element.15), channel_id=1, source_target_pairs={{0,24},{2,26},{4,28},{6,30},{8,0},{10,2},{12,4},{14,6},{16,8},{18,... | collective-permute-start | bytes 786440 | tf_op jit(solution)/shard_map/ppermute | solution.py:12
  52.9 9.1 %collective-permute-start.1 = (f32[1,256,4]{2,1,0:T(8,128)S(1)}, f32[1,256,4]{2,1,0:T(8,128)S(1)}, u32[]{:S(2)}, u32[]{:S(2)}) collective-permute-start(f32[1,256,4]{2,1,0:T(8,128)S(1)} %get-tuple-element.37), channel_id=1, source_target_pairs={{0,2},{2,4},{4,6},{6,8},{8,10},{10,12},{12,14},{14,16},{16,18},{18... | collective-permute-start | bytes 12296 | tf_op jit(solution)/shard_map/ppermute | solution.py:21
  52.9 9.0 %collective-permute-start.2 = (f32[1,256,4]{2,1,0:T(8,128)S(1)}, f32[1,256,4]{2,1,0:T(8,128)S(1)}, u32[]{:S(2)}, u32[]{:S(2)}) collective-permute-start(f32[1,256,4]{2,1,0:T(8,128)S(1)} %get-tuple-element.38), channel_id=1, source_target_pairs={{2,0},{4,2},{6,4},{8,6},{10,8},{12,10},{14,12},{16,14},{18,16},{20... | collective-permute-start | bytes 12296 | tf_op jit(solution)/shard_map/ppermute | solution.py:24
  57.5 7.2 %collective-permute-start.4 = (f32[1,256,4]{2,1,0:T(8,128)S(1)}, f32[1,256,4]{2,1,0:T(8,128)S(1)}, u32[]{:S(2)}, u32[]{:S(2)}) collective-permute-start(f32[1,256,4]{2,1,0:T(8,128)S(1)} %get-tuple-element.39), channel_id=1, source_target_pairs={{0,2},{2,4},{4,6},{6,8},{8,10},{10,12},{12,14},{14,16},{16,18},{18... | collective-permute-start | bytes 12296 | tf_op jit(solution)/shard_map/ppermute | solution.py:21
  57.5 7.2 %collective-permute-start.5 = (f32[1,256,4]{2,1,0:T(8,128)S(1)}, f32[1,256,4]{2,1,0:T(8,128)S(1)}, u32[]{:S(2)}, u32[]{:S(2)}) collective-permute-start(f32[1,256,4]{2,1,0:T(8,128)S(1)} %get-tuple-element.40), channel_id=1, source_target_pairs={{2,0},{4,2},{6,4},{8,6},{10,8},{12,10},{14,12},{16,14},{18,16},{20... | collective-permute-start | bytes 12296 | tf_op jit(solution)/shard_map/ppermute | solution.py:24
Sparse Core Ops, SparseCore 0:
  10.9 31.4 all-reduce.4
where the time goes:
time: 85.1 us; the launch traced here: 84.2 us
  waiting for transfers between devices  39.7 us (47%)
  other arithmetic  14.6 us (17%)
  between operations  14.1 us (17%)
  starting transfers between devices  12.9 us (15%)
  local copies, waits for them, and re-layouts  2.83 us (3%)
    psum x1, waiting for transfers between devices, from_root(): return lax.psum(jnp.where(mine, shard, jnp.zeros_like(shard)), axis)  32.1 us
    another operation x3, other arithmetic, per_device(): jacobian = jnp.stack(state[2:6])[None]  10.5 us
    ppermute x2, starting transfers between devices, extended(): lax.ppermute(lax.slice_in_dim(block, 0, width, axis=dim), axis, backward)  8.86 us
    ppermute x2, waiting for transfers between devices, shifted(): return lax.ppermute(value, axis, pairs)  5.06 us
    ppermute x2, starting transfers between devices, shifted(): return lax.ppermute(value, axis, pairs)  3.92 us
    ppermute x2, waiting for transfers between devices, extended(): lax.ppermute(lax.slice_in_dim(block, block.shape[dim] - width, None, axis...  2.54 us
    unnamed x8, local copies, waits for them, and re-layouts  2.06 us
    select_n x1, other arithmetic, from_root(): return lax.psum(jnp.where(mine, shard, jnp.zeros_like(shard)), axis)  1.78 us
  transfers between devices with their start and end apart: 7, of which 3 were waited for; matrix products, arithmetic and copies ran while one was open for 1% of the time, Pallas kernels for 0%

commit v1 on v0

v1 whole, which is shorter than its diff:
```python
import functools

import jax
import jax.numpy as jnp
from jax import lax
from jax.experimental import pallas as pl
from jax.experimental.pallas import tpu as pltpu
from jax.sharding import PartitionSpec as P

LANES = 128
PACK = 8
CHUNKS = 8
GROUP = 16


def exchange_kernel(
    planes, count, turn,
    pot, shift, weight, scale,
    sky, halo, params,
    tile, low_pack, high_pack, strips, columns,
    load_sem, turn_send, turn_recv, plane_send, plane_recv, halo_send, halo_recv,
):
    me = lax.axis_index("lon")
    own = lax.axis_index("plane")
    rows = pot.shape[1]
    step = rows // CHUNKS

    def at(moves, plane):
        return {"lon": lax.rem(me + moves + count, count), "plane": plane}

    others = [lax.rem(own + d, planes) for d in range(1, planes)]
    load = pltpu.make_async_copy(pot.at[0], tile, load_sem)
    load.start()

    barrier = pltpu.get_barrier_semaphore()
    senders = [at(turn, own)] + [at(0, q) for q in others]
    senders += [at(turn + side, q) for side in (-1, 1) for q in [own] + others]
    for device in senders:
        pl.semaphore_signal(
            barrier, inc=1, device_id=device, device_id_type=pl.DeviceIdType.MESH
        )
    pl.semaphore_wait(barrier, len(senders))

    turned = []
    for k in range(CHUNKS):
        part = pl.ds(k * step, step)
        copy = pltpu.make_async_remote_copy(
            src_ref=pot.at[0, part],
            dst_ref=sky.at[own, part],
            send_sem=turn_send.at[k],
            recv_sem=turn_recv.at[k],
            device_id=at(-turn, own),
            device_id_type=pl.DeviceIdType.MESH,
        )
        copy.start()
        turned.append(copy)

    load.wait()
    low_pack[...] = jnp.transpose(tile[:, :LANES])[:PACK]
    high_pack[...] = jnp.transpose(tile[:, tile.shape[1] - LANES :])[LANES - PACK :]
    edges = []
    for i, q in enumerate([own] + others):
        for side, (source, first, moves) in enumerate(
            ((low_pack, 0, -turn - 1), (high_pack, LANES - PACK, -turn + 1))
        ):
            copy = pltpu.make_async_remote_copy(
                src_ref=source,
                dst_ref=strips.at[own, pl.ds(first, PACK)],
                send_sem=halo_send.at[i, side],
                recv_sem=halo_recv.at[own, side],
                device_id=at(moves, q),
                device_id_type=pl.DeviceIdType.MESH,
            )
            copy.start()
            edges.append(copy)

    columns[...] = jnp.zeros_like(columns)
    columns[0:2] = shift[...].astype(jnp.float32)
    columns[2:4] = weight[...].astype(jnp.float32) / 16.0
    columns[4:5] = scale[...].reshape(1, rows)
    params[...] = jnp.transpose(columns[...])
    strips[:, PACK : LANES - PACK] = jnp.zeros(
        (planes, LANES - 2 * PACK, rows), jnp.float32
    )

    handed = []
    for k in range(CHUNKS):
        part = pl.ds(k * step, step)
        turned[k].wait_recv()
        for i, q in enumerate(others):
            copy = pltpu.make_async_remote_copy(
                src_ref=sky.at[own, part],
                dst_ref=sky.at[own, part],
                send_sem=plane_send.at[i, k],
                recv_sem=plane_recv.at[own, k],
                device_id=at(0, q),
                device_id_type=pl.DeviceIdType.MESH,
            )
            copy.start()
            handed.append(copy)

    for q in [own] + others:
        for side, (source, first) in enumerate(((low_pack, 0), (high_pack, LANES - PACK))):
            pltpu.make_async_remote_copy(
                src_ref=source,
                dst_ref=strips.at[q, pl.ds(first, PACK)],
                send_sem=halo_send.at[0, side],
                recv_sem=halo_recv.at[q, side],
                device_id=at(0, others[0]),
                device_id_type=pl.DeviceIdType.MESH,
            ).wait_recv()
    for k in range(planes):
        halo[k] = jnp.transpose(strips[k])

    for q in others:
        for k in range(CHUNKS):
            part = pl.ds(k * step, step)
            pltpu.make_async_remote_copy(
                src_ref=sky.at[q, part],
                dst_ref=sky.at[q, part],
                send_sem=plane_send.at[0, k],
                recv_sem=plane_recv.at[q, k],
                device_id=at(0, others[0]),
                device_id_type=pl.DeviceIdType.MESH,
            ).wait_recv()
    for copy in turned + edges + handed:
        copy.wait_send()


def ray_kernel(planes, gains, sky, halo, params, disp, jac, disp_buf, jac_buf, out_sem):
    rows = sky.shape[1]
    blocks = sky.shape[2] // LANES
    total = blocks + 1
    lane = lax.broadcasted_iota(jnp.int32, (GROUP, LANES), 1)
    row = lax.broadcasted_iota(jnp.int32, (GROUP, LANES), 0)

    def right(parts):
        turned = [pltpu.roll(part, LANES - 1, 1) for part in parts]
        return [
            jnp.where(lane == LANES - 1, turned[(v + 1) % total], turned[v])
            for v in range(total)
        ]

    def left(parts):
        turned = [pltpu.roll(part, 1, 1) for part in parts]
        return [jnp.where(lane == 0, turned[v - 1], turned[v]) for v in range(total)]

    def load(k, start, stop):
        parts = [sky[k, start:stop, v * LANES : (v + 1) * LANES] for v in range(blocks)]
        return parts + [halo[k, start:stop, :]]

    copies = []
    for g in range(rows // GROUP):
        start, stop = g * GROUP, (g + 1) * GROUP
        column = [
            jnp.broadcast_to(params[start:stop, i : i + 1], (GROUP, LANES)) for i in range(5)
        ]
        metric = column[4]
        stencils = []
        for side in range(2):
            place = lane + column[side].astype(jnp.int32)
            frac = column[2 + side]
            stencils.append((place & (LANES - 1), place < 0, place >= LANES, frac, 1.0 - frac))
        state = [None] * blocks
        for k in range(planes):
            gain = gains[0, k]
            here = load(k, start, stop)
            if g == 0:
                above = [jnp.where(row == 0, 0.0, pltpu.roll(part, 1, 0)) for part in here]
            else:
                above = load(k, start - 1, stop - 1)
            if stop == rows:
                below = [
                    jnp.where(row == GROUP - 1, 0.0, pltpu.roll(part, GROUP - 1, 0))
                    for part in here
                ]
            else:
                below = load(k, start + 1, stop + 1)
            values = []
            for (place, under, over, frac, rest), parts in zip(stencils, (above, below)):
                mixed = [rest * a + frac * b for a, b in zip(parts, right(parts))]
                picked = [jnp.take_along_axis(part, place, axis=1) for part in mixed]
                values.append(
                    [
                        jnp.where(
                            under,
                            picked[v - 1],
                            jnp.where(over, picked[(v + 1) % total], picked[v]),
                        )
                        for v in range(total)
                    ]
                )
            north, south = values
            slope = [s - n for s, n in zip(south, north)]
            slope_right, slope_left = right(slope), left(slope)
            here_right, here_left = right(here), left(here)
            for v in range(blocks):
                alpha_t = 0.5 * slope[v]
                alpha_p = 0.5 * metric * (here_right[v] - here_left[v])
                u_tt = south[v] - 2.0 * here[v] + north[v]
                u_pp = metric * metric * (here_right[v] - 2.0 * here[v] + here_left[v])
                u_tp = 0.25 * metric * (slope_right[v] - slope_left[v])
                if k == 0:
                    off = -gain * u_tp
                    state[v] = (
                        -gain * alpha_t, -gain * alpha_p,
                        1.0 - gain * u_tt, off, off, 1.0 - gain * u_pp,
                    )
                else:
                    d_t, d_p, zz, zo, oz, oo = state[v]
                    state[v] = (
                        d_t - gain * (alpha_t + u_tt * d_t + u_tp * d_p),
                        d_p - gain * (alpha_p + u_tp * d_t + u_pp * d_p),
                        zz - gain * (u_tt * zz + u_tp * oz),
                        zo - gain * (u_tt * zo + u_tp * oo),
                        oz - gain * (u_tp * zz + u_pp * oz),
                        oo - gain * (u_tp * zo + u_pp * oo),
                    )
        for v in range(blocks):
            part = pl.ds(v * LANES, LANES)
            for i in range(2):
                disp_buf[i, start:stop, part] = state[v][i]
            for i in range(4):
                jac_buf[i, start:stop, part] = state[v][2 + i]
        here = pl.ds(start, GROUP)
        for i, (source, target) in enumerate(((disp_buf, disp), (jac_buf, jac))):
            copy = pltpu.make_async_copy(
                source.at[:, here], target.at[0, :, here], out_sem.at[i, g]
            )
            copy.start()
            copies.append(copy)
    for copy in copies:
        copy.wait()


def per_device(planes, count, potential, lens_weight, cycle_shift, cycle_weight, cycle_scale):
    rows, width = potential.shape[1:]
    f32 = jnp.float32
    vmem = pl.BlockSpec(memory_space=pltpu.VMEM)
    anywhere = pl.BlockSpec(memory_space=pl.ANY)
    dma = pltpu.SemaphoreType.DMA
    sky, halo, params = pl.pallas_call(
        functools.partial(exchange_kernel, planes, count, count // 4),
        out_shape=(
            jax.ShapeDtypeStruct((planes, rows, width), f32),
            jax.ShapeDtypeStruct((planes, rows, LANES), f32),
            jax.ShapeDtypeStruct((rows, LANES), f32),
        ),
        in_specs=[anywhere, vmem, vmem, vmem],
        out_specs=(vmem, vmem, vmem),
        scratch_shapes=[
            pltpu.VMEM((rows, width), f32),
            pltpu.VMEM((PACK, rows), f32),
            pltpu.VMEM((PACK, rows), f32),
            pltpu.VMEM((planes, LANES, rows), f32),
            pltpu.VMEM((LANES, rows), f32),
            dma,
            dma((CHUNKS,)),
            dma((CHUNKS,)),
            dma((planes - 1, CHUNKS)),
            dma((planes, CHUNKS)),
            dma((planes, 2)),
            dma((planes, 2)),
        ],
        compiler_params=pltpu.CompilerParams(
            collective_id=0, has_side_effects=True, vmem_limit_bytes=32 * 2**20
        ),
        name="exchange",
    )(potential, cycle_shift, cycle_weight, cycle_scale)
    return tuple(
        pl.pallas_call(
            functools.partial(ray_kernel, planes),
            out_shape=(
                jax.ShapeDtypeStruct((1, 2, rows, width), f32),
                jax.ShapeDtypeStruct((1, 4, rows, width), f32),
            ),
            in_specs=[pl.BlockSpec(memory_space=pltpu.SMEM), vmem, vmem, vmem],
            out_specs=(anywhere, anywhere),
            scratch_shapes=[
                pltpu.VMEM((2, rows, width), f32),
                pltpu.VMEM((4, rows, width), f32),
                dma((2, rows // GROUP)),
            ],
            compiler_params=pltpu.CompilerParams(vmem_limit_bytes=32 * 2**20),
            name="rays",
        )(lens_weight, sky, halo, params)
    )


def solution(mesh):
    in_specs = (P("plane", None, "lon"), P("plane", None), P(), P(), P())
    out_specs = (P("plane", None, None, "lon"), P("plane", None, None, "lon"))
    return jax.shard_map(
        functools.partial(per_device, mesh.shape["plane"], mesh.shape["lon"]),
        mesh=mesh, in_specs=in_specs, out_specs=out_specs, check_vma=False,
    )
```

time: 85.1 us -> 29.8 us (0.35)
  waiting for transfers between devices: 39.7 us -> 0 us
  Pallas kernels: 0 us -> 25.2 us
  other arithmetic: 14.6 us -> 0 us
  between operations: 14.1 us -> 0.66 us
  starting transfers between devices: 12.9 us -> 0 us
    psum x1 -> x0, waiting for transfers between devices: 32.1 us -> none  [from_root(): return lax.psum(jnp.where(mine, shard, jnp.zeros_like(shard)), axis)]
    pallas_call x0 -> x2, Pallas kernels: none -> 25.2 us  [the longest x1 15.3 us: per_device(): pl.pallas_call(functools.partial(exchange_kernel, planes, count, count //...]
    ppermute x6 -> x0, starting transfers between devices: 12.9 us -> none  [the longest x2 8.86 us: extended(): lax.ppermute(lax.slice_in_dim(block, 0, width, axis=dim), axis, backward)]
    another operation x3 -> x0, other arithmetic: 10.5 us -> none  [per_device(): jacobian = jnp.stack(state[2:6])[None]]
    ppermute x6 -> x0, waiting for transfers between devices: 7.6 us -> none  [the longest x2 5.06 us: shifted(): return lax.ppermute(value, axis, pairs)]
    broadcast_in_dim x2 -> x0, other arithmetic: 1.87 us -> none  [the longest x1 1.04 us: per_device(): jacobian = jnp.stack(state[2:6])[None]]
    select_n x1 -> x0, other arithmetic: 1.78 us -> none  [from_root(): return lax.psum(jnp.where(mine, shard, jnp.zeros_like(shard)), axis)]
    unnamed x8 -> x10, local copies, waits for them, and re-layouts: 2.06 us -> 3.63 us
  transfers between devices with their start and end apart: 7 -> 0, of which waited for: 3 -> 0; matrix products, arithmetic and copies ran while one was open for 1% -> 0% of each run, Pallas kernels for 0% -> 0%
where the time goes in v1:
time: 29.8 us; the launch traced here: 29.5 us
  Pallas kernels  25.2 us (85%)
  local copies, waits for them, and re-layouts  3.63 us (12%)
  between operations  0.66 us (2%)
    pallas_call x1, Pallas kernels, per_device(): pl.pallas_call(functools.partial(exchange_kernel, planes, count, count //...  15.3 us
    pallas_call x1, Pallas kernels, per_device(): pl.pallas_call(functools.partial(ray_kernel, planes), out_shape=(jax.Shap...  9.9 us
    unnamed x10, local copies, waits for them, and re-layouts  3.63 us

profile of v1, /device:TPU:0, one launch (start us, length us, event | category | flops | bytes accessed | tf_op | source)
XLA Modules:
  0.0 29.5 jit_solution(17637379060727000698)
XLA Ops:
  0.6 0.0 copy-start
  0.6 0.9 %copy-done = f32[1,256,256]{2,1,0:T(8,128)S(1)} copy-done((f32[1,256,256]{2,1,0:T(8,128)S(1)}, f32[1,256,256]{2,1,0:T(8,128)}, u32[]{:S(2)}) %copy-start) | copy-done | bytes 262168
  1.6 0.0 copy-start.1
  1.6 0.7 %copy-done.1 = s32[2,256]{1,0:T(2,128)S(1)} copy-done((s32[2,256]{1,0:T(2,128)S(1)}, s32[2,256]{1,0:T(2,128)}, u32[]{:S(2)}) %copy-start.1) | copy-done | bytes 2072
  2.3 0.0 copy-start.2
  2.3 0.7 %copy-done.2 = s32[2,256]{1,0:T(2,128)S(1)} copy-done((s32[2,256]{1,0:T(2,128)S(1)}, s32[2,256]{1,0:T(2,128)}, u32[]{:S(2)}) %copy-start.2) | copy-done | bytes 2072
  2.9 0.0 copy-start.3
  2.9 0.7 %copy-done.3 = f32[256]{0:T(256)S(1)} copy-done((f32[256]{0:T(256)S(1)}, f32[256]{0:T(256)}, u32[]{:S(2)}) %copy-start.3) | copy-done | bytes 1048
  3.6 15.3 %exchange.1 = (f32[2,256,256]{2,1,0:T(8,128)S(1)}, f32[2,256,128]{2,1,0:T(8,128)S(1)}, f32[256,128]{1,0:T(8,128)S(1)}) custom-call(f32[1,256,256]{2,1,0:T(8,128)S(1)} %copy-done, s32[2,256]{1,0:T(2,128)S(1)} %copy-done.1, s32[2,256]{1,0:T(2,128)S(1)} %copy-done.2, f32[256]{0:T(256)S(1)} %copy-done.3), custom_call_target="tpu_custom_call" | custom-call | tf_op jit(solution)/shard_map/exchange/pallas_call | solution.py:242
  19.0 0.0 copy-start.4
  19.0 0.6 %copy-done.4 = f32[1,2]{1,0:T(1,128)S(1)} copy-done((f32[1,2]{1,0:T(1,128)S(1)}, f32[1,2]{1,0:T(1,128)}, u32[]{:S(2)}) %copy-start.4) | copy-done | bytes 32
  19.6 9.9 %rays.1 = (f32[1,2,256,256]{3,2,1,0:T(8,128)}, f32[1,4,256,256]{3,2,1,0:T(8,128)}) custom-call(f32[1,2]{1,0:T(1,128)S(1)} %copy-done.4, f32[2,256,256]{2,1,0:T(8,128)S(1)} %get-tuple-element.5.sky, f32[2,256,128]{2,1,0:T(8,128)S(1)} %get-tuple-element.6.halo, f32[256,128]{1,0:T(8,128)S(1)} %get-tuple-element.7.params), custom_call_target="tpu_custom_call" | custom-call | tf_op jit(solution)/shard_map/rays/pallas_call | solution.py:271
Async XLA Ops:
  0.6 1.0 %copy-start = (f32[1,256,256]{2,1,0:T(8,128)S(1)}, f32[1,256,256]{2,1,0:T(8,128)}, u32[]{:S(2)}) copy-start(f32[1,256,256]{2,1,0:T(8,128)} %pot.1) | copy-start | bytes 786436
  1.6 0.7 %copy-start.1 = (s32[2,256]{1,0:T(2,128)S(1)}, s32[2,256]{1,0:T(2,128)}, u32[]{:S(2)}) copy-start(s32[2,256]{1,0:T(2,128)} %shift.1) | copy-start | bytes 6148
  2.3 0.7 %copy-start.2 = (s32[2,256]{1,0:T(2,128)S(1)}, s32[2,256]{1,0:T(2,128)}, u32[]{:S(2)}) copy-start(s32[2,256]{1,0:T(2,128)} %weight.1) | copy-start | bytes 6148
  2.9 0.7 %copy-start.3 = (f32[256]{0:T(256)S(1)}, f32[256]{0:T(256)}, u32[]{:S(2)}) copy-start(f32[256]{0:T(256)} %scale.1) | copy-start | bytes 3076
  19.0 0.7 %copy-start.4 = (f32[1,2]{1,0:T(1,128)S(1)}, f32[1,2]{1,0:T(1,128)}, u32[]{:S(2)}) copy-start(f32[1,2]{1,0:T(1,128)} %gains.1) | copy-start | bytes 28

commit v2 on v1

--- a/solution.py
+++ b/solution.py
@@ -10,14 +10,15 @@
 LANES = 128
 PACK = 8
 CHUNKS = 8
-GROUP = 16
+GROUP = 32
+WINDOW = 3
 
 
 def exchange_kernel(
     planes, count, turn,
-    pot, shift, weight, scale,
+    pot, gains_hbm, shift_hbm, weight_hbm, scale_hbm,
     sky, halo, params,
-    tile, low_pack, high_pack, strips, columns,
+    tile, gains, shift, weight, scale, low_pack, high_pack, strips, columns,
     load_sem, turn_send, turn_recv, plane_send, plane_recv, halo_send, halo_recv,
 ):
     me = lax.axis_index("lon")
@@ -29,8 +30,17 @@
         return {"lon": lax.rem(me + moves + count, count), "plane": plane}
 
     others = [lax.rem(own + d, planes) for d in range(1, planes)]
-    load = pltpu.make_async_copy(pot.at[0], tile, load_sem)
-    load.start()
+    loads = [
+        pltpu.make_async_copy(source, target, load_sem.at[i])
+        for i, (source, target) in enumerate(
+            (
+                (pot.at[0], tile), (gains_hbm, gains), (shift_hbm, shift),
+                (weight_hbm, weight), (scale_hbm, scale),
+            )
+        )
+    ]
+    for load in loads:
+        load.start()
 
     barrier = pltpu.get_barrier_semaphore()
     senders = [at(turn, own)] + [at(0, q) for q in others]
@@ -52,10 +62,12 @@
             device_id=at(-turn, own),
             device_id_type=pl.DeviceIdType.MESH,
         )
+        turned.append(copy)
+    for copy in turned[:WINDOW]:
         copy.start()
-        turned.append(copy)
-
-    load.wait()
+
+    for load in loads:
+        load.wait()
     low_pack[...] = jnp.transpose(tile[:, :LANES])[:PACK]
     high_pack[...] = jnp.transpose(tile[:, tile.shape[1] - LANES :])[LANES - PACK :]
     edges = []
@@ -78,6 +90,8 @@
     columns[0:2] = shift[...].astype(jnp.float32)
     columns[2:4] = weight[...].astype(jnp.float32) / 16.0
     columns[4:5] = scale[...].reshape(1, rows)
+    for k in range(planes):
+        columns[5 + k : 6 + k] = jnp.full((1, rows), gains[0, k], jnp.float32)
     params[...] = jnp.transpose(columns[...])
     strips[:, PACK : LANES - PACK] = jnp.zeros(
         (planes, LANES - 2 * PACK, rows), jnp.float32
@@ -86,6 +100,9 @@
     handed = []
     for k in range(CHUNKS):
         part = pl.ds(k * step, step)
+        if k + WINDOW < CHUNKS:
+            turned[k].wait_send()
+            turned[k + WINDOW].start()
         turned[k].wait_recv()
         for i, q in enumerate(others):
             copy = pltpu.make_async_remote_copy(
@@ -123,11 +140,11 @@
                 device_id=at(0, others[0]),
                 device_id_type=pl.DeviceIdType.MESH,
             ).wait_recv()
-    for copy in turned + edges + handed:
+    for copy in turned[CHUNKS - WINDOW :] + edges + handed:
         copy.wait_send()
 
 
-def ray_kernel(planes, gains, sky, halo, params, disp, jac, disp_buf, jac_buf, out_sem):
+def ray_kernel(planes, sky, halo, params, disp, jac, disp_buf, jac_buf, out_sem):
     rows = sky.shape[1]
     blocks = sky.shape[2] // LANES
     total = blocks + 1
@@ -153,7 +170,8 @@
     for g in range(rows // GROUP):
         start, stop = g * GROUP, (g + 1) * GROUP
         column = [
-            jnp.broadcast_to(params[start:stop, i : i + 1], (GROUP, LANES)) for i in range(5)
+            jnp.broadcast_to(params[start:stop, i : i + 1], (GROUP, LANES))
+            for i in range(5 + planes)
         ]
         metric = column[4]
         stencils = []
@@ -163,7 +181,7 @@
             stencils.append((place & (LANES - 1), place < 0, place >= LANES, frac, 1.0 - frac))
         state = [None] * blocks
         for k in range(planes):
-            gain = gains[0, k]
+            gain = column[5 + k]
             here = load(k, start, stop)
             if g == 0:
                 above = [jnp.where(row == 0, 0.0, pltpu.roll(part, 1, 0)) for part in here]
@@ -238,6 +256,7 @@
     f32 = jnp.float32
     vmem = pl.BlockSpec(memory_space=pltpu.VMEM)
     anywhere = pl.BlockSpec(memory_space=pl.ANY)
+    hbm = pl.BlockSpec(memory_space=pltpu.HBM)
     dma = pltpu.SemaphoreType.DMA
     sky, halo, params = pl.pallas_call(
         functools.partial(exchange_kernel, planes, count, count // 4),
@@ -246,15 +265,19 @@
             jax.ShapeDtypeStruct((planes, rows, LANES), f32),
             jax.ShapeDtypeStruct((rows, LANES), f32),
         ),
-        in_specs=[anywhere, vmem, vmem, vmem],
+        in_specs=[hbm] * 5,
         out_specs=(vmem, vmem, vmem),
         scratch_shapes=[
             pltpu.VMEM((rows, width), f32),
+            pltpu.SMEM((1, planes), f32),
+            pltpu.VMEM((2, rows), jnp.int32),
+            pltpu.VMEM((2, rows), jnp.int32),
+            pltpu.VMEM((rows,), f32),
             pltpu.VMEM((PACK, rows), f32),
             pltpu.VMEM((PACK, rows), f32),
             pltpu.VMEM((planes, LANES, rows), f32),
             pltpu.VMEM((LANES, rows), f32),
-            dma,
+            dma((5,)),
             dma((CHUNKS,)),
             dma((CHUNKS,)),
             dma((planes - 1, CHUNKS)),
@@ -266,7 +289,7 @@
             collective_id=0, has_side_effects=True, vmem_limit_bytes=32 * 2**20
         ),
         name="exchange",
-    )(potential, cycle_shift, cycle_weight, cycle_scale)
+    )(potential, lens_weight, cycle_shift, cycle_weight, cycle_scale)
     return tuple(
         pl.pallas_call(
             functools.partial(ray_kernel, planes),
@@ -274,7 +297,7 @@
                 jax.ShapeDtypeStruct((1, 2, rows, width), f32),
                 jax.ShapeDtypeStruct((1, 4, rows, width), f32),
             ),
-            in_specs=[pl.BlockSpec(memory_space=pltpu.SMEM), vmem, vmem, vmem],
+            in_specs=[vmem, vmem, vmem],
             out_specs=(anywhere, anywhere),
             scratch_shapes=[
                 pltpu.VMEM((2, rows, width), f32),
@@ -283,7 +306,7 @@
             ],
             compiler_params=pltpu.CompilerParams(vmem_limit_bytes=32 * 2**20),
             name="rays",
-        )(lens_weight, sky, halo, params)
+        )(sky, halo, params)
     )
 
 

time: 29.8 us -> 27.8 us (0.933)
  Pallas kernels: 25.2 us -> 23.3 us
    pallas_call x1, Pallas kernels: 9.9 us -> 6.62 us  [per_device(): pl.pallas_call(functools.partial(ray_kernel, planes), out_shape=(jax.Shap...]
    pallas_call x1, Pallas kernels: 15.3 us -> 16.6 us  [per_device(): pl.pallas_call(functools.partial(exchange_kernel, planes, count, count //...]
where the time goes in v2:
time: 27.8 us; the launch traced here: 27.5 us
  Pallas kernels  23.3 us (84%)
  local copies, waits for them, and re-layouts  3.64 us (13%)
  between operations  0.65 us (2%)
    pallas_call x1, Pallas kernels, per_device(): pl.pallas_call(functools.partial(exchange_kernel, planes, count, count //...  16.6 us
    pallas_call x1, Pallas kernels, per_device(): pl.pallas_call(functools.partial(ray_kernel, planes), out_shape=(jax.Shap...  6.62 us
    unnamed x10, local copies, waits for them, and re-layouts  3.64 us

profile of v2, /device:TPU:0, one launch (start us, length us, event | category | flops | bytes accessed | tf_op | source)
XLA Modules:
  0.0 27.5 jit_solution(3201831226179404432)
XLA Ops:
  0.6 0.0 copy-start
  0.6 0.9 %copy-done = f32[1,256,256]{2,1,0:T(8,128)S(1)} copy-done((f32[1,256,256]{2,1,0:T(8,128)S(1)}, f32[1,256,256]{2,1,0:T(8,128)}, u32[]{:S(2)}) %copy-start) | copy-done | bytes 262168
  1.6 0.0 copy-start.1
  1.6 0.7 %copy-done.1 = s32[2,256]{1,0:T(2,128)S(1)} copy-done((s32[2,256]{1,0:T(2,128)S(1)}, s32[2,256]{1,0:T(2,128)}, u32[]{:S(2)}) %copy-start.1) | copy-done | bytes 2072
  2.3 0.0 copy-start.2
  2.3 0.7 %copy-done.2 = s32[2,256]{1,0:T(2,128)S(1)} copy-done((s32[2,256]{1,0:T(2,128)S(1)}, s32[2,256]{1,0:T(2,128)}, u32[]{:S(2)}) %copy-start.2) | copy-done | bytes 2072
  2.9 0.0 copy-start.3
  2.9 0.7 %copy-done.3 = f32[256]{0:T(256)S(1)} copy-done((f32[256]{0:T(256)S(1)}, f32[256]{0:T(256)}, u32[]{:S(2)}) %copy-start.3) | copy-done | bytes 1048
  3.6 0.0 copy-start.4
  3.6 0.7 %copy-done.4 = f32[1,2]{1,0:T(1,128)S(1)} copy-done((f32[1,2]{1,0:T(1,128)S(1)}, f32[1,2]{1,0:T(1,128)}, u32[]{:S(2)}) %copy-start.4) | copy-done | bytes 32
  4.3 16.6 %exchange.1 = (f32[2,256,256]{2,1,0:T(8,128)S(1)}, f32[2,256,128]{2,1,0:T(8,128)S(1)}, f32[256,128]{1,0:T(8,128)S(1)}) custom-call(f32[1,256,256]{2,1,0:T(8,128)S(1)} %copy-done, f32[1,2]{1,0:T(1,128)S(1)} %copy-done.4, s32[2,256]{1,0:T(2,128)S(1)} %copy-done.1, s32[2,256]{1,0:T(2,128)S(1)} %copy-done.2, f32[256]{0:T(256)S(1)} %copy-done.3), custom_call_target="tpu_custom_call" | custom-call | tf_op jit(solution)/shard_map/exchange/pallas_call | solution.py:261
  20.9 6.6 %rays.1 = (f32[1,2,256,256]{3,2,1,0:T(8,128)}, f32[1,4,256,256]{3,2,1,0:T(8,128)}) custom-call(f32[2,256,256]{2,1,0:T(8,128)S(1)} %get-tuple-element.5.sky, f32[2,256,128]{2,1,0:T(8,128)S(1)} %get-tuple-element.6.halo, f32[256,128]{1,0:T(8,128)S(1)} %get-tuple-element.7.params), custom_call_target="tpu_custom_call" | custom-call | tf_op jit(solution)/shard_map/rays/pallas_call | solution.py:294
Async XLA Ops:
  0.6 1.0 %copy-start = (f32[1,256,256]{2,1,0:T(8,128)S(1)}, f32[1,256,256]{2,1,0:T(8,128)}, u32[]{:S(2)}) copy-start(f32[1,256,256]{2,1,0:T(8,128)} %pot.1) | copy-start | bytes 786436
  1.6 0.7 %copy-start.1 = (s32[2,256]{1,0:T(2,128)S(1)}, s32[2,256]{1,0:T(2,128)}, u32[]{:S(2)}) copy-start(s32[2,256]{1,0:T(2,128)} %shift_hbm.1) | copy-start | bytes 6148
  2.3 0.7 %copy-start.2 = (s32[2,256]{1,0:T(2,128)S(1)}, s32[2,256]{1,0:T(2,128)}, u32[]{:S(2)}) copy-start(s32[2,256]{1,0:T(2,128)} %weight_hbm.1) | copy-start | bytes 6148
  2.9 0.7 %copy-start.3 = (f32[256]{0:T(256)S(1)}, f32[256]{0:T(256)}, u32[]{:S(2)}) copy-start(f32[256]{0:T(256)} %scale_hbm.1) | copy-start | bytes 3076
  3.6 0.7 %copy-start.4 = (f32[1,2]{1,0:T(1,128)S(1)}, f32[1,2]{1,0:T(1,128)}, u32[]{:S(2)}) copy-start(f32[1,2]{1,0:T(1,128)} %gains_hbm.1) | copy-start | bytes 28

commit v3 on v2

v3 whole, which is shorter than its diff:
```python
import functools

import jax
import jax.numpy as jnp
from jax import lax
from jax.experimental import pallas as pl
from jax.experimental.pallas import tpu as pltpu
from jax.sharding import PartitionSpec as P

LANES = 128
PACK = 8
CHUNKS = 8
LAG = 2


def lens_kernel(
    planes, count, turn,
    pot, gains_hbm, shift_hbm, weight_hbm, scale_hbm,
    disp, jac,
    sky, halo, params, fields, disp_buf, jac_buf, tile, gains, shift, weight, scale, low_pack, high_pack, strips, columns,
    load_sem, turn_send, turn_recv, plane_send, plane_recv, halo_send, halo_recv, out_sem,
):
    me = lax.axis_index("lon")
    own = lax.axis_index("plane")
    rows = pot.shape[1]
    step = rows // CHUNKS

    def at(moves, plane):
        return {"lon": lax.rem(me + moves + count, count), "plane": plane}

    others = [lax.rem(own + d, planes) for d in range(1, planes)]
    loads = [
        pltpu.make_async_copy(source, target, load_sem.at[i])
        for i, (source, target) in enumerate(
            (
                (pot.at[0], tile), (gains_hbm, gains), (shift_hbm, shift),
                (weight_hbm, weight), (scale_hbm, scale),
            )
        )
    ]
    for load in loads:
        load.start()

    barrier = pltpu.get_barrier_semaphore()
    senders = [at(turn, own)] + [at(0, q) for q in others]
    senders += [at(turn + side, q) for side in (-1, 1) for q in [own] + others]
    for device in senders:
        pl.semaphore_signal(
            barrier, inc=1, device_id=device, device_id_type=pl.DeviceIdType.MESH
        )
    pl.semaphore_wait(barrier, len(senders))

    turned = []
    for k in range(CHUNKS):
        part = pl.ds(k * step, step)
        copy = pltpu.make_async_remote_copy(
            src_ref=pot.at[0, part],
            dst_ref=sky.at[own, part],
            send_sem=turn_send.at[k],
            recv_sem=turn_recv.at[k],
            device_id=at(-turn, own),
            device_id_type=pl.DeviceIdType.MESH,
        )
        copy.start()
        turned.append(copy)

    for load in loads:
        load.wait()
    low_pack[...] = jnp.transpose(tile[:, :LANES])[:PACK]
    high_pack[...] = jnp.transpose(tile[:, tile.shape[1] - LANES :])[LANES - PACK :]
    edges = []
    for i, q in enumerate([own] + others):
        for side, (source, first, moves) in enumerate(
            ((low_pack, 0, -turn - 1), (high_pack, LANES - PACK, -turn + 1))
        ):
            copy = pltpu.make_async_remote_copy(
                src_ref=source,
                dst_ref=strips.at[own, pl.ds(first, PACK)],
                send_sem=halo_send.at[i, side],
                recv_sem=halo_recv.at[own, side],
                device_id=at(moves, q),
                device_id_type=pl.DeviceIdType.MESH,
            )
            copy.start()
            edges.append(copy)

    columns[...] = jnp.zeros_like(columns)
    columns[0:2] = shift[...].astype(jnp.float32)
    columns[2:4] = weight[...].astype(jnp.float32) / 16.0
    columns[4:5] = scale[...].reshape(1, rows)
    params[...] = jnp.transpose(columns[...])
    strips[:, PACK : LANES - PACK] = jnp.zeros(
        (planes, LANES - 2 * PACK, rows), jnp.float32
    )

    lane = lax.broadcasted_iota(jnp.int32, (step, LANES), 1)
    row = lax.broadcasted_iota(jnp.int32, (step, LANES), 0)
    blocks = sky.shape[2] // LANES
    total = blocks + 1

    def right(parts):
        turns = [pltpu.roll(part, LANES - 1, 1) for part in parts]
        return [
            jnp.where(lane == LANES - 1, turns[(v + 1) % total], turns[v])
            for v in range(total)
        ]

    def left(parts):
        turns = [pltpu.roll(part, 1, 1) for part in parts]
        return [jnp.where(lane == 0, turns[v - 1], turns[v]) for v in range(total)]

    def column(g, i):
        return jnp.broadcast_to(params[g * step : (g + 1) * step, i : i + 1], (step, LANES))

    def load(k, start, stop):
        parts = [sky[k, start:stop, v * LANES : (v + 1) * LANES] for v in range(blocks)]
        return parts + [halo[k, start:stop, :]]

    def derive(k, g):
        start, stop = g * step, (g + 1) * step
        metric = column(g, 4)
        here = load(k, start, stop)
        if g == 0:
            above = [jnp.where(row == 0, 0.0, pltpu.roll(part, 1, 0)) for part in here]
        else:
            above = load(k, start - 1, stop - 1)
        if stop == rows:
            below = [jnp.where(row == step - 1, 0.0, pltpu.roll(part, step - 1, 0)) for part in here]
        else:
            below = load(k, start + 1, stop + 1)
        values = []
        for side, parts in enumerate((above, below)):
            spot = lane + column(g, side).astype(jnp.int32)
            place = spot & (LANES - 1)
            under, over = spot < 0, spot >= LANES
            frac = column(g, 2 + side)
            rest = 1.0 - frac
            mixed = [rest * a + frac * b for a, b in zip(parts, right(parts))]
            picked = [jnp.take_along_axis(part, place, axis=1) for part in mixed]
            values.append(
                [
                    jnp.where(
                        under,
                        picked[v - 1],
                        jnp.where(over, picked[(v + 1) % total], picked[v]),
                    )
                    for v in range(total)
                ]
            )
        north, south = values
        slope = [s - n for s, n in zip(south, north)]
        slope_right, slope_left = right(slope), left(slope)
        here_right, here_left = right(here), left(here)
        for v in range(blocks):
            found = (
                0.5 * slope[v],
                0.5 * metric * (here_right[v] - here_left[v]),
                south[v] - 2.0 * here[v] + north[v],
                metric * metric * (here_right[v] - 2.0 * here[v] + here_left[v]),
                0.25 * metric * (slope_right[v] - slope_left[v]),
            )
            for i, field in enumerate(found):
                fields[k, i, start:stop, v * LANES : (v + 1) * LANES] = field

    written = []

    def trace(g):
        start, stop = g * step, (g + 1) * step
        for v in range(blocks):
            part = slice(v * LANES, (v + 1) * LANES)
            for k in range(planes):
                gain = gains[0, k]
                alpha_t, alpha_p, u_tt, u_pp, u_tp = [
                    fields[k, i, start:stop, part] for i in range(5)
                ]
                if k == 0:
                    off = -gain * u_tp
                    d_t, d_p = -gain * alpha_t, -gain * alpha_p
                    zz, zo, oz, oo = 1.0 - gain * u_tt, off, off, 1.0 - gain * u_pp
                else:
                    d_t, d_p, zz, zo, oz, oo = (
                        d_t - gain * (alpha_t + u_tt * d_t + u_tp * d_p),
                        d_p - gain * (alpha_p + u_tp * d_t + u_pp * d_p),
                        zz - gain * (u_tt * zz + u_tp * oz),
                        zo - gain * (u_tt * zo + u_tp * oo),
                        oz - gain * (u_tp * zz + u_pp * oz),
                        oo - gain * (u_tp * zo + u_pp * oo),
                    )
            for i, value in enumerate((d_t, d_p)):
                disp_buf[i, start:stop, part] = value
            for i, value in enumerate((zz, zo, oz, oo)):
                jac_buf[i, start:stop, part] = value
        for i, (source, target) in enumerate(((disp_buf, disp), (jac_buf, jac))):
            copy = pltpu.make_async_copy(
                source.at[:, pl.ds(start, step)],
                target.at[0, :, pl.ds(start, step)],
                out_sem.at[i, g],
            )
            copy.start()
            written.append(copy)

    def edges_arrive(q):
        for side, (source, first) in enumerate(((low_pack, 0), (high_pack, LANES - PACK))):
            pltpu.make_async_remote_copy(
                src_ref=source,
                dst_ref=strips.at[q, pl.ds(first, PACK)],
                send_sem=halo_send.at[0, side],
                recv_sem=halo_recv.at[q, side],
                device_id=at(0, others[0]),
                device_id_type=pl.DeviceIdType.MESH,
            ).wait_recv()
        halo[q] = jnp.transpose(strips[q])

    handed = []
    for k in range(CHUNKS + 1 + LAG):
        if k < CHUNKS:
            part = pl.ds(k * step, step)
            turned[k].wait_recv()
            for i, q in enumerate(others):
                copy = pltpu.make_async_remote_copy(
                    src_ref=sky.at[own, part],
                    dst_ref=sky.at[own, part],
                    send_sem=plane_send.at[i, k],
                    recv_sem=plane_recv.at[own, k],
                    device_id=at(0, q),
                    device_id_type=pl.DeviceIdType.MESH,
                )
                copy.start()
                handed.append(copy)
        if k == 0:
            edges_arrive(own)
        if 1 <= k <= CHUNKS:
            derive(own, k - 1)
        late = k - LAG
        if 0 <= late < CHUNKS:
            for q in others:
                part = pl.ds(late * step, step)
                pltpu.make_async_remote_copy(
                    src_ref=sky.at[q, part],
                    dst_ref=sky.at[q, part],
                    send_sem=plane_send.at[0, late],
                    recv_sem=plane_recv.at[q, late],
                    device_id=at(0, others[0]),
                    device_id_type=pl.DeviceIdType.MESH,
                ).wait_recv()
                if late == 0:
                    edges_arrive(q)
        if 1 <= late:
            for q in others:
                derive(q, late - 1)
            trace(late - 1)
    for copy in turned + edges + handed:
        copy.wait_send()
    for copy in written:
        copy.wait()


def per_device(planes, count, potential, lens_weight, cycle_shift, cycle_weight, cycle_scale):
    rows, width = potential.shape[1:]
    f32 = jnp.float32
    anywhere = pl.BlockSpec(memory_space=pl.ANY)
    dma = pltpu.SemaphoreType.DMA
    return tuple(
        pl.pallas_call(
            functools.partial(lens_kernel, planes, count, count // 4),
            out_shape=(
                jax.ShapeDtypeStruct((1, 2, rows, width), f32),
                jax.ShapeDtypeStruct((1, 4, rows, width), f32),
            ),
            in_specs=[anywhere] * 5,
            out_specs=(anywhere, anywhere),
            scratch_shapes=[
                pltpu.VMEM((planes, rows, width), f32),
                pltpu.VMEM((planes, rows, LANES), f32),
                pltpu.VMEM((rows, LANES), f32),
                pltpu.VMEM((planes, 5, rows, width), f32),
                pltpu.VMEM((2, rows, width), f32),
                pltpu.VMEM((4, rows, width), f32),
                pltpu.VMEM((rows, width), f32),
                pltpu.SMEM((1, planes), f32),
                pltpu.VMEM((2, rows), jnp.int32),
                pltpu.VMEM((2, rows), jnp.int32),
                pltpu.VMEM((rows,), f32),
                pltpu.VMEM((PACK, rows), f32),
                pltpu.VMEM((PACK, rows), f32),
                pltpu.VMEM((planes, LANES, rows), f32),
                pltpu.VMEM((LANES, rows), f32),
                dma((5,)),
                dma((CHUNKS,)),
                dma((CHUNKS,)),
                dma((planes - 1, CHUNKS)),
                dma((planes, CHUNKS)),
                dma((planes, 2)),
                dma((planes, 2)),
                dma((2, CHUNKS)),
            ],
            compiler_params=pltpu.CompilerParams(
                collective_id=0, has_side_effects=True, vmem_limit_bytes=60 * 2**20
            ),
            name="lens",
        )(potential, lens_weight, cycle_shift, cycle_weight, cycle_scale)
    )


def solution(mesh):
    in_specs = (P("plane", None, "lon"), P("plane", None), P(), P(), P())
    out_specs = (P("plane", None, None, "lon"), P("plane", None, None, "lon"))
    return jax.shard_map(
        functools.partial(per_device, mesh.shape["plane"], mesh.shape["lon"]),
        mesh=mesh, in_specs=in_specs, out_specs=out_specs, check_vma=False,
    )
```

time: 27.8 us -> 27.8 us (level)
  the two profiles are of different devices: /device:TPU:0 before, /device:TPU:24 now
where the time goes in v3:
time: 27.8 us; the launch traced here: 27.6 us
  Pallas kernels  24.1 us (87%)
  local copies, waits for them, and re-layouts  2.93 us (11%)
  between operations  0.65 us (2%)
    pallas_call x1, Pallas kernels, per_device(): pl.pallas_call(functools.partial(lens_kernel, planes, count, count // 4),...  24.1 us
    unnamed x4, local copies, waits for them, and re-layouts  2.93 us

profile of v3, /device:TPU:24, one launch (start us, length us, event | category | flops | bytes accessed | tf_op | source)
XLA Modules:
  0.0 27.6 jit_solution(3005752340961382871)
XLA Ops:
  0.6 24.1 %lens.1 = (f32[1,2,256,256]{3,2,1,0:T(8,128)}, f32[1,4,256,256]{3,2,1,0:T(8,128)}) custom-call(f32[1,256,256]{2,1,0:T(8,128)} %pot.1, f32[1,2]{1,0:T(1,128)} %gains_hbm.1, s32[2,256]{1,0:T(2,128)} %shift_hbm.1, s32[2,256]{1,0:T(2,128)} %weight_hbm.1, f32[256]{0:T(256)} %scale_hbm.1), custom_call_target="tpu_custom_call" | custom-call | tf_op jit(solution)/shard_map/lens/pallas_call | solution.py:264
  24.7 0.0 copy-start
  24.7 2.0 %copy.9 = f32[1,2,256,256]{3,2,1,0:T(8,128)} copy(f32[1,2,256,256]{3,2,1,0:T(8,128)} %get-tuple-element.4) | data formatting | bytes 1048576
  26.7 0.0 copy-done
  26.7 1.0 %copy.10 = f32[1,4,256,256]{3,2,1,0:T(8,128)} copy(f32[1,4,256,256]{3,2,1,0:T(8,128)S(1)} %copy-done) | data formatting | bytes 2097152
Async XLA Ops:
  24.7 2.0 %copy-start = (f32[1,4,256,256]{3,2,1,0:T(8,128)S(1)}, f32[1,4,256,256]{3,2,1,0:T(8,128)}, u32[]{:S(2)}) copy-start(f32[1,4,256,256]{3,2,1,0:T(8,128)} %get-tuple-element.5) | copy-start | bytes 3145732

commit v4 on v3

--- a/solution.py
+++ b/solution.py
@@ -9,7 +9,7 @@
 
 LANES = 128
 PACK = 8
-CHUNKS = 8
+CHUNKS = 4
 LAG = 2
 
 
@@ -61,8 +61,9 @@
             device_id=at(-turn, own),
             device_id_type=pl.DeviceIdType.MESH,
         )
+        turned.append(copy)
+    for copy in turned[: CHUNKS // 2]:
         copy.start()
-        turned.append(copy)
 
     for load in loads:
         load.wait()
@@ -83,6 +84,7 @@
             )
             copy.start()
             edges.append(copy)
+    turned[CHUNKS // 2].start()
 
     columns[...] = jnp.zeros_like(columns)
     columns[0:2] = shift[...].astype(jnp.float32)
@@ -93,6 +95,8 @@
         (planes, LANES - 2 * PACK, rows), jnp.float32
     )
 
+    for copy in turned[CHUNKS // 2 + 1 :]:
+        copy.start()
     lane = lax.broadcasted_iota(jnp.int32, (step, LANES), 1)
     row = lax.broadcasted_iota(jnp.int32, (step, LANES), 0)
     blocks = sky.shape[2] // LANES

time: 27.8 us -> 23.3 us (0.84)
  the two profiles are of different devices: /device:TPU:24 before, /device:TPU:0 now
where the time goes in v4:
time: 23.3 us; the launch traced here: 23.2 us
  Pallas kernels  19.6 us (84%)
  local copies, waits for them, and re-layouts  2.93 us (13%)
  between operations  0.65 us (3%)
    pallas_call x1, Pallas kernels, per_device(): pl.pallas_call(functools.partial(lens_kernel, planes, count, count // 4),...  19.6 us
    unnamed x4, local copies, waits for them, and re-layouts  2.93 us

profile of v4, /device:TPU:0, one launch (start us, length us, event | category | flops | bytes accessed | tf_op | source)
XLA Modules:
  0.0 23.2 jit_solution(2296318194183199303)
XLA Ops:
  0.6 19.6 %lens.1 = (f32[1,2,256,256]{3,2,1,0:T(8,128)}, f32[1,4,256,256]{3,2,1,0:T(8,128)}) custom-call(f32[1,256,256]{2,1,0:T(8,128)} %pot.1, f32[1,2]{1,0:T(1,128)} %gains_hbm.1, s32[2,256]{1,0:T(2,128)} %shift_hbm.1, s32[2,256]{1,0:T(2,128)} %weight_hbm.1, f32[256]{0:T(256)} %scale_hbm.1), custom_call_target="tpu_custom_call" | custom-call | tf_op jit(solution)/shard_map/lens/pallas_call | solution.py:268
  20.2 0.0 copy-start
  20.3 2.0 %copy.9 = f32[1,2,256,256]{3,2,1,0:T(8,128)} copy(f32[1,2,256,256]{3,2,1,0:T(8,128)} %get-tuple-element.4) | data formatting | bytes 1048576
  22.2 0.0 copy-done
  22.2 1.0 %copy.10 = f32[1,4,256,256]{3,2,1,0:T(8,128)} copy(f32[1,4,256,256]{3,2,1,0:T(8,128)S(1)} %copy-done) | data formatting | bytes 2097152
Async XLA Ops:
  20.2 2.0 %copy-start = (f32[1,4,256,256]{3,2,1,0:T(8,128)S(1)}, f32[1,4,256,256]{3,2,1,0:T(8,128)}, u32[]{:S(2)}) copy-start(f32[1,4,256,256]{3,2,1,0:T(8,128)} %get-tuple-element.5) | copy-start | bytes 3145732

commit v5 on v4

--- a/solution.py
+++ b/solution.py
@@ -10,7 +10,7 @@
 LANES = 128
 PACK = 8
 CHUNKS = 4
-LAG = 2
+LAG = 3
 
 
 def lens_kernel(

time: 23.3 us -> 23.3 us (level)
  no operation moved by 1% of the time
where the time goes in v5:
time: 23.3 us; the launch traced here: 23.2 us
  Pallas kernels  19.6 us (84%)
  local copies, waits for them, and re-layouts  2.93 us (13%)
  between operations  0.65 us (3%)
    pallas_call x1, Pallas kernels, per_device(): pl.pallas_call(functools.partial(lens_kernel, planes, count, count // 4),...  19.6 us
    unnamed x4, local copies, waits for them, and re-layouts  2.93 us

profile of v5, /device:TPU:0, one launch (start us, length us, event | category | flops | bytes accessed | tf_op | source)
XLA Modules:
  0.0 23.2 jit_solution(11824508445220415502)
XLA Ops:
  0.6 19.6 %lens.1 = (f32[1,2,256,256]{3,2,1,0:T(8,128)}, f32[1,4,256,256]{3,2,1,0:T(8,128)}) custom-call(f32[1,256,256]{2,1,0:T(8,128)} %pot.1, f32[1,2]{1,0:T(1,128)} %gains_hbm.1, s32[2,256]{1,0:T(2,128)} %shift_hbm.1, s32[2,256]{1,0:T(2,128)} %weight_hbm.1, f32[256]{0:T(256)} %scale_hbm.1), custom_call_target="tpu_custom_call" | custom-call | tf_op jit(solution)/shard_map/lens/pallas_call | solution.py:268
  20.2 0.0 copy-start
  20.3 2.0 %copy.9 = f32[1,2,256,256]{3,2,1,0:T(8,128)} copy(f32[1,2,256,256]{3,2,1,0:T(8,128)} %get-tuple-element.4) | data formatting | bytes 1048576
  22.2 0.0 copy-done
  22.2 1.0 %copy.10 = f32[1,4,256,256]{3,2,1,0:T(8,128)} copy(f32[1,4,256,256]{3,2,1,0:T(8,128)S(1)} %copy-done) | data formatting | bytes 2097152
Async XLA Ops:
  20.2 2.0 %copy-start = (f32[1,4,256,256]{3,2,1,0:T(8,128)S(1)}, f32[1,4,256,256]{3,2,1,0:T(8,128)}, u32[]{:S(2)}) copy-start(f32[1,4,256,256]{3,2,1,0:T(8,128)} %get-tuple-element.5) | copy-start | bytes 3145732
